TPU v7x, 128 devices: a whole 4x4x4 slice. The times are simulated.
128 devices in a mesh: row: 8 (over y, core), col: 16 (over x, z).
Axes of the slice: x: 4, y: 4, z: 4, core: 2. Of those that a mesh axis runs over, the one named last changes fastest.
Arguments:
- speech: bfloat16 [8192, 1024], P(('row', 'col')), may hold values from -16 to 16
- speech_mass: float32 [8192], P(('row', 'col')), may hold values from 0.2 to 15
- text: bfloat16 [16384, 1024], P('col', 'row'), may hold values from -16 to 16
- text_mass: float32 [16384], P('col'), may hold values from 0.2 to 15
Outputs:
- cross: float32 [1024, 1024], P(('row', 'col'))
- speech_potential: float32 [8192], P('row')
- text_potential: float32 [16384], P('col')
All inputs are finite; a program needn't handle non-finite values.
Results may differ from a plain program's by a relative error of at most 0.015.
Values may be sent and summed in bfloat16 or wider, within the bound.
No kernel may reach another device: no remote copies, remote signals or barrier semaphores. Data moves between devices by JAX's collectives and lax.ppermute only.
A program may use at most 64 MiB of HBM per device.

v0:
```python
import functools
import math

import jax
import jax.numpy as jnp
from jax import lax
from jax.experimental import pallas as pl
from jax.experimental.pallas import tpu as pltpu
from jax.sharding import PartitionSpec as P

ITERS = 3
EPS = 0.5
LANES = 128
SUB = 8
LOG2E = math.log2(math.e)
LIMIT = 24 * 1024 * 1024


def call(kernel, outs, scratch=(), flops=0, reads=0, args=0, aliases={}):
    vmem = pl.BlockSpec(memory_space=pltpu.VMEM)
    return pl.pallas_call(
        kernel,
        out_shape=outs,
        in_specs=[vmem] * args,
        out_specs=[vmem] * len(outs),
        scratch_shapes=list(scratch),
        input_output_aliases=aliases,
        compiler_params=pltpu.CompilerParams(vmem_limit_bytes=LIMIT),
        cost_estimate=pl.CostEstimate(flops=flops, bytes_accessed=reads, transcendentals=0),
    )


def f32(*shape):
    return jax.ShapeDtypeStruct(shape, jnp.float32)


def bf16(*shape):
    return jax.ShapeDtypeStruct(shape, jnp.bfloat16)


def total_of(x):
    return jnp.sum(jnp.sum(x, axis=1, keepdims=True), axis=0, keepdims=True)


def combine(got_ref):
    tops = got_ref[:, 0:SUB, :]
    best = jnp.max(tops, axis=0)
    mass = jnp.sum(got_ref[:, SUB : 2 * SUB, :] * jnp.exp2(tops - best[None]), axis=0)
    whole = jnp.sum(got_ref[:, 2 * SUB : 3 * SUB, :], axis=0)
    return best, mass, whole


def send(out_ref, top, mass, whole):
    whole = jnp.broadcast_to(whole, (SUB, LANES))
    for peer in range(out_ref.shape[0]):
        out_ref[peer, 0:SUB, :] = top
        out_ref[peer, SUB : 2 * SUB, :] = mass
        out_ref[peer, 2 * SUB : 3 * SUB, :] = whole


def spread(v, out_ref):
    turned = jnp.concatenate([v, jnp.zeros((LANES - SUB, LANES), jnp.float32)], axis=0).T
    for b in range(SUB):
        out_ref[b * LANES : (b + 1) * LANES, :] = jnp.broadcast_to(
            turned[:, b : b + 1], (LANES, LANES)
        )


def column_stats(scores_ref, rows_ref, top_ref, mass_ref):
    for b in range(SUB):
        values = scores_ref[:, b * LANES : (b + 1) * LANES] + rows_ref[...]
        top = jnp.max(values, axis=0, keepdims=True)
        top_ref[b : b + 1, :] = top
        mass_ref[b : b + 1, :] = jnp.sum(jnp.exp2(values - top), axis=0, keepdims=True)


def row_stats(scores_ref, v, use=None):
    lane = lax.broadcasted_iota(jnp.int32, (LANES, LANES), 1)
    shift = jnp.concatenate([v[b : b + 1, :] for b in range(SUB)], axis=1)
    both = jnp.zeros((LANES, LANES), jnp.float32)
    for b in range(SUB):
        values = scores_ref[b * LANES : (b + 1) * LANES, :] + shift
        top = jnp.max(values, axis=1, keepdims=True)
        weights = jnp.exp2(values - top)
        mass = jnp.sum(weights, axis=1, keepdims=True)
        both = jnp.where(lane == b, top, both)
        both = jnp.where(lane == SUB + b, mass, both)
        if use is not None:
            use(b, weights)
    turned = both.T
    return turned[0:SUB, :], turned[SUB : 2 * SUB, :]


def pack_kernel(speech_ref, mass_ref, piece_ref):
    rows, width = speech_ref.shape
    blocks = width // LANES
    rest = jnp.concatenate([mass_ref[...], mass_ref[...]], axis=1)
    line = lax.broadcasted_iota(jnp.int32, (16, LANES), 0)
    tail = jnp.zeros((16, LANES), jnp.float32)
    for k in range(3):
        term = rest.astype(jnp.bfloat16).astype(jnp.float32)
        tail = jnp.where(line == k, term, tail)
        rest = rest - term
    for lt in range(blocks):
        piece_ref[lt * rows : (lt + 1) * rows, :] = speech_ref[:, lt * LANES : (lt + 1) * LANES]
    piece_ref[blocks * rows :, :] = tail.astype(jnp.bfloat16)


def place_kernel(*refs):
    slice_refs, t_ref = refs[:-1], refs[-1]
    here = lax.axis_index("row")
    blocks = t_ref.shape[0]
    chips = blocks // 2
    for k in range(blocks):
        t_ref[lax.rem(here // 2 + chips - k // 2, chips) * 2 + lax.rem(here + k, 2)] = slice_refs[k][...]


def join_kernel(*refs):
    for k, piece_ref in enumerate(refs[:-1]):
        refs[-1][k] = piece_ref[...]


def lines_kernel(scale, rows, steps, first, last, *refs):
    line_refs, t_ref, refs = refs[: len(steps)], refs[len(steps)], refs[len(steps) + 1 :]
    if first:
        held_ref, stats_ref = None, None
    else:
        held_ref, stats_ref = refs[2:4]
        refs = refs[4:]
    if last:
        scores_ref, s_ref, mass_ref, out_ref, new_held_ref, new_stats_ref, column_ref = refs
    else:
        scores_ref, s_ref, new_held_ref, new_stats_ref, column_ref = refs
    side = line_refs[0].shape[0]
    blocks = t_ref.shape[0]
    core = lax.rem(lax.axis_index("row"), 2)
    here = lax.axis_index("col")
    x, z = here // side, lax.rem(here, side)
    lane = lax.broadcasted_iota(jnp.int32, (1, LANES), 1)
    base = blocks * rows

    def origin(step, k):
        back_x = step + core * (k - step)
        back_z = k + core * (step - k)
        return lax.rem(x + side - back_x, side) * side + lax.rem(z + side - back_z, side)

    pieces = [
        (origin(step, k), line_ref.at[k])
        for step, line_ref in zip(steps, line_refs, strict=True)
        for k in range(side)
    ]
    if not first:
        new_held_ref[...] = held_ref[...]
    masses = []
    for c, piece_ref in pieces:
        terms = piece_ref[base : base + 16, :].astype(jnp.float32)
        masses.append(terms[0:1, :] + terms[1:2, :] + terms[2:3, :])
        new_held_ref[pl.ds(c, 1), :] = masses[-1]
        place = pl.ds(pl.multiple_of(c * rows, rows), rows)
        for lt in range(blocks):
            s_ref[lt, place, :] = piece_ref[lt * rows : (lt + 1) * rows, :]
    empty = jnp.zeros((LANES - len(pieces), LANES), jnp.float32)
    turned = jnp.concatenate([jnp.log2(jnp.concatenate(masses, axis=0)), empty], axis=0).T
    for k in range(len(pieces)):
        column_ref[k * rows : (k + 1) * rows, :] = jnp.broadcast_to(
            turned[0:rows, k : k + 1], (rows, LANES)
        )
    whole = jnp.concatenate(
        [
            jnp.concatenate(
                [piece_ref[lt * rows : (lt + 1) * rows, :] for _, piece_ref in pieces], axis=0
            )
            for lt in range(blocks)
        ],
        axis=1,
    )
    for n in range(4):
        text = jnp.concatenate([t_ref[lt, n * 256 : (n + 1) * 256, :] for lt in range(blocks)], axis=1)
        product = scale * lax.dot_general(
            whole, text, (((1,), (1,)), ((), ())), preferred_element_type=jnp.float32
        )
        for k, (c, _) in enumerate(pieces):
            place = pl.ds(pl.multiple_of(c * rows, rows), rows)
            scores_ref[place, n * 256 : (n + 1) * 256] = product[k * rows : (k + 1) * rows, :]
        for b in (2 * n, 2 * n + 1):
            values = product[:, (b - 2 * n) * LANES : (b - 2 * n + 1) * LANES] + column_ref[...]
            top = jnp.max(values, axis=0, keepdims=True)
            mass = jnp.sum(jnp.exp2(values - top), axis=0, keepdims=True)
            if not first:
                old_top, old_mass = stats_ref[b : b + 1, :], stats_ref[SUB + b : SUB + b + 1, :]
                best = jnp.maximum(top, old_top)
                mass = mass * jnp.exp2(top - best) + old_mass * jnp.exp2(old_top - best)
                top = best
            new_stats_ref[b : b + 1, :] = top
            new_stats_ref[SUB + b : SUB + b + 1, :] = mass
    if last:
        for b in range(SUB):
            mass_ref[b : b + 1, :] = jnp.where(
                lane < rows, new_held_ref[2 * b : 2 * b + 1, :], new_held_ref[2 * b + 1 : 2 * b + 2, :]
            )
        send(out_ref, new_stats_ref[0:SUB, :], new_stats_ref[SUB : 2 * SUB, :], total_of(mass_ref[...]))


def row_kernel(got_ref, scores_ref, mass_ref, out_ref):
    best, mass, whole = combine(got_ref)
    dual = jnp.log2(whole) - (best + jnp.log2(mass))
    top, mass = row_stats(scores_ref, dual + jnp.log2(mass_ref[...]))
    send(out_ref, top, mass, total_of(mass_ref[...]))


def last_row_kernel(
    got_ref, scores_ref, mass_ref, t_ref, out_ref, raw_ref, dual_ref, *weights_refs
):
    best, mass, whole = combine(got_ref)
    dual = jnp.log2(whole) - (best + jnp.log2(mass))
    dual_ref[...] = dual * (EPS / LOG2E)

    text = jnp.concatenate([t_ref[lt] for lt in range(t_ref.shape[0])], axis=1)


    def product(k):
        raw_ref[k * 256 : (k + 1) * 256, :] = jnp.dot(
            weights_refs[k][...], text, preferred_element_type=jnp.float32
        )

    def use(b, weights):
        rows = slice((b % 2) * LANES, (b % 2 + 1) * LANES)
        weights_refs[b // 2][rows, :] = weights.astype(jnp.bfloat16)
        if b % 2 == 1 and b > 1:
            product(b // 2 - 1)

    top, mass = row_stats(scores_ref, dual + jnp.log2(mass_ref[...]), use)
    product(3)
    send(out_ref, top, mass, total_of(mass_ref[...]))


def column_kernel(got_ref, scores_ref, mass_ref, out_ref, rows_ref, a_ref, b_ref):
    best, mass, whole = combine(got_ref)
    dual = jnp.log2(whole) - (best + jnp.log2(mass))
    spread(dual + jnp.log2(mass_ref[...]), rows_ref)
    column_stats(scores_ref, rows_ref, a_ref, b_ref)
    send(out_ref, a_ref[...], b_ref[...], total_of(mass_ref[...]))


def half_cross(s_ref, part, carried):
    left = jnp.concatenate([s_ref[2 * k + part] for k in range(s_ref.shape[0] // 2)], axis=1)
    return lax.dot_general(
        left, carried, (((0,), (0,)), ((), ())), preferred_element_type=jnp.float32
    )


def first_cross_kernel(
    got_ref, sent_ref, row_got_ref, mass_ref, raw_ref, s_ref,
    carried_ref, other_ref, dual_ref, rows_ref,
):
    best, mass, whole = combine(got_ref)
    dual_ref[...] = (jnp.log2(whole) - (best + jnp.log2(mass))) * (EPS / LOG2E)
    speech_total = jnp.sum(row_got_ref[:, 2 * SUB : 3 * SUB, :], axis=0)
    factor = (mass_ref[...] / speech_total) * jnp.exp2(sent_ref[0, 0:SUB, :] - best) / mass
    spread(factor, rows_ref)
    part = 1 - lax.rem(lax.axis_index("row"), 2)

    def product(n):
        lanes = slice(n * 256, (n + 1) * 256)
        other_ref[:, lanes] = half_cross(s_ref, part, carried_ref[:, lanes]).astype(jnp.bfloat16)

    for n in range(4):
        for b in (2 * n, 2 * n + 1):
            carried_ref[:, b * LANES : (b + 1) * LANES] = (
                raw_ref[:, b * LANES : (b + 1) * LANES] * rows_ref[...]
            ).astype(jnp.bfloat16)
        if n > 0:
            product(n - 1)
    product(3)


def second_cross_kernel(carried_ref, s_ref, out_ref):
    out_ref[...] = half_cross(s_ref, lax.rem(lax.axis_index("row"), 2), carried_ref[...])


def pair_kernel(mine_ref, other_ref, out_ref):
    out_ref[...] = (mine_ref[...] + other_ref[...].astype(jnp.float32)).astype(jnp.bfloat16)


def body(speech, speech_mass, text, text_mass):
    rows, width = speech.shape
    columns, row_count = lax.axis_size("col"), lax.axis_size("row")
    cores = 2
    blocks = width // LANES
    big = columns * rows
    flops = 2 * big * big * width

    swap = [(i, i ^ 1) for i in range(row_count)]

    def back(v, k):
        return lax.ppermute(v, "row", [(i, (i + cores * k) % row_count) for i in range(row_count)])

    piece_rows = blocks * rows + 16
    side = 4

    def shift(v, k, swapped):
        moves = []
        for r in range(row_count):
            for x in range(side):
                for z in range(side):
                    to = (x, (z + k) % side) if r % cores == swapped else ((x + k) % side, z)
                    moves.append((r * columns + x * side + z, r * columns + to[0] * side + to[1]))
        return lax.ppermute(v, ("row", "col"), moves)

    (piece,) = call(pack_kernel, [bf16(piece_rows, LANES)], args=2)(
        speech, speech_mass.reshape(1, rows)
    )
    pieces = [piece] + [shift(piece, k, 0) for k in range(1, side)]
    beside = back(text, 1), back(text, 3)
    (line,) = call(join_kernel, [bf16(side, piece_rows, LANES)], args=side)(*pieces)
    late, line = lax.optimization_barrier((text, line))
    lines = [line] + [shift(line, k, 1) for k in range(1, side)]
    slices = [late, beside[0], back(late, 2), beside[1]]
    slices = [v for piece in slices for v in (piece, lax.ppermute(piece, "row", swap))]
    column_mass = text_mass.reshape(SUB, LANES)

    scale = LOG2E / (math.sqrt(width) * EPS)
    vector = pltpu.VMEM((SUB, LANES), jnp.float32)
    column = pltpu.VMEM((big, LANES), jnp.float32)
    (t,) = call(
        place_kernel, [bf16(blocks, big, LANES)], args=row_count
    )(*slices)
    grown = [f32(big, big), bf16(blocks, big, LANES)]
    small = [f32(columns, LANES), f32(2 * SUB, LANES)]
    held = call(
        functools.partial(lines_kernel, scale, rows, (0,), True, False),
        grown + small,
        [pltpu.VMEM((big // side, LANES), jnp.float32)],
        args=2,
    )(lines[0], t)
    held = call(
        functools.partial(lines_kernel, scale, rows, (1, 3), False, False),
        grown + small,
        [pltpu.VMEM((big // 2, LANES), jnp.float32)],
        args=7,
        aliases={3: 0, 4: 1},
    )(lines[1], lines[3], t, *held)
    scores, s, row_mass, piece = call(
        functools.partial(lines_kernel, scale, rows, (2,), False, True),
        grown + [f32(SUB, LANES), f32(row_count, 24, LANES)],
        [pltpu.VMEM(v.shape, v.dtype) for v in small]
        + [pltpu.VMEM((big // side, LANES), jnp.float32)],
        flops=flops // side,
        args=6,
        aliases={2: 0, 3: 1},
    )(lines[2], t, *held)
    row_swap = lambda v: lax.all_to_all(v, "row", 0, 0)
    column_swap = lambda v: lax.all_to_all(v, "col", 0, 0)
    for step in range(ITERS):
        got_row = row_swap(piece)
        if step < ITERS - 1:
            (piece,) = call(row_kernel, [f32(columns, 24, LANES)], args=3)(
                got_row, scores, column_mass
            )
            got = column_swap(piece)
            (piece,) = call(
                column_kernel, [f32(row_count, 24, LANES)], [column, vector, vector], args=3
            )(got, scores, row_mass)
    sent, raw, text_dual = call(
        last_row_kernel,
        [f32(columns, 24, LANES), f32(big, width), f32(SUB, LANES)],
        [pltpu.VMEM((big // 4, big), jnp.bfloat16)] * 4,
        flops=flops,
        args=4,
    )(got_row, scores, column_mass, t)
    got = column_swap(sent)
    carried, other, speech_dual = call(
        first_cross_kernel,
        [bf16(big, width), bf16(width // 2, width), f32(SUB, LANES)],
        [column],
        flops=flops // 2,
        args=6,
    )(got, sent, got_row, row_mass, raw, s)
    other = lax.ppermute(other, "row", swap)
    (mine,) = call(second_cross_kernel, [f32(width // 2, width)], flops=flops // 2, args=2)(
        carried, s
    )
    (pair,) = call(pair_kernel, [bf16(width // 2, width)], args=2)(mine, other)
    groups = [
        [r * columns + c for r in range(core, row_count, cores) for c in range(columns)]
        for core in range(cores)
    ]
    count = len(groups[0])
    parts = lax.all_to_all(
        pair.reshape(count, width // 2 // count, width),
        ("row", "col"),
        0,
        0,
        axis_index_groups=groups,
    )
    cross = jnp.sum(parts.astype(jnp.float32), axis=0) * math.sqrt(big * row_count)
    return (cross, speech_dual.reshape(-1), text_dual.reshape(-1))


def solution(mesh):
    return jax.shard_map(
        body,
        mesh=mesh,
        in_specs=(P(("row", "col"), None), P(("row", "col")), P("col", "row"), P("col")),
        out_specs=(P(("row", "col"), None), P("row"), P("col")),
        check_vma=False,
    )
```

profile of v0, /device:TPU:0, one launch (start us, length us, event | category | flops | bytes accessed | tf_op | source)
XLA Modules:
  0.0 135.7 jit_solution(14481240025024811200)
XLA Ops:
  2.3 4.1 %collective-permute-start.2 = (bf16[528,128]{1,0:T(8,128)(2,1)S(1)}, bf16[528,128]{1,0:T(8,128)(2,1)S(1)}, u32[]{:S(2)}, u32[]{:S(2)}) collective-permute-start(bf16[528,128]{1,0:T(8,128)(2,1)S(1)} %shard_map.67.refs_0_), channel_id=1, source_target_pairs={{0,3},{1,0},{2,1},{3,2},{4,7},{5,4},{6,5},{7,6},{8,11},{9,8},{10,9... | collective-permute-start | bytes 405512 | tf_op jit(solution)/shard_map/ppermute | solution.py:308
  6.4 1.3 collective-permute-start
  7.7 3.0 %collective-permute-start.9 = (bf16[1024,128]{1,0:T(8,128)(2,1)}, bf16[1024,128]{1,0:T(8,128)(2,1)S(1)}, u32[]{:S(2)}, u32[]{:S(2)}) collective-permute-start(bf16[1024,128]{1,0:T(8,128)(2,1)} %refs_0_), channel_id=1, source_target_pairs={{0,96},{16,112},{32,0},{48,16},{64,32},{80,48},{96,64},{112,80},{1... | collective-permute-start | bytes 786440 | tf_op jit(solution)/shard_map/ppermute | solution.py:296
  10.7 2.3 %collective-permute-done.1.refs_2_ = bf16[528,128]{1,0:T(8,128)(2,1)S(1)} collective-permute-done((bf16[528,128]{1,0:T(8,128)(2,1)S(1)}, bf16[528,128]{1,0:T(8,128)(2,1)S(1)}, u32[]{:S(2)}, u32[]{:S(2)}) %collective-permute-start.1) | collective-permute-done | bytes 135200 | tf_op jit(solution)/shard_map/ppermute | solution.py:308
  14.1 3.3 %collective-permute-start.7 = (bf16[1024,128]{1,0:T(8,128)(2,1)}, bf16[1024,128]{1,0:T(8,128)(2,1)S(1)}, u32[]{:S(2)}, u32[]{:S(2)}) collective-permute-start(bf16[1024,128]{1,0:T(8,128)(2,1)} %refs_0_), channel_id=1, source_target_pairs={{0,64},{16,80},{32,96},{48,112},{64,0},{80,16},{96,32},{112,48},{1... | collective-permute-start | bytes 786440 | tf_op jit(solution)/shard_map/ppermute | solution.py:296
  17.4 2.8 %collective-permute-start.12 = (bf16[4,528,128]{2,1,0:T(8,128)(2,1)S(1)}, bf16[4,528,128]{2,1,0:T(8,128)(2,1)S(1)}, u32[]{:S(2)}, u32[]{:S(2)}) collective-permute-start(bf16[4,528,128]{2,1,0:T(8,128)(2,1)S(1)} %shard_map.68.refs_0_), channel_id=1, source_target_pairs={{0,12},{1,13},{2,14},{3,15},{4,0},{5,1},{6,2},{7,3},{8,4},{9,5},{1... | collective-permute-start | bytes 1622024 | tf_op jit(solution)/shard_map/ppermute | solution.py:308
  20.2 2.3 %collective-permute-start.3 = (bf16[4,528,128]{2,1,0:T(8,128)(2,1)S(1)}, bf16[4,528,128]{2,1,0:T(8,128)(2,1)S(1)}, u32[]{:S(2)}, u32[]{:S(2)}) collective-permute-start(bf16[4,528,128]{2,1,0:T(8,128)(2,1)S(1)} %shard_map.68.refs_0_), channel_id=1, source_target_pairs={{0,8},{1,9},{2,10},{3,11},{4,12},{5,13},{6,14},{7,15},{8,0},{9,1},... | collective-permute-start | bytes 1622024 | tf_op jit(solution)/shard_map/ppermute | solution.py:308
  22.5 1.6 %collective-permute-done.5.refs_2_ = bf16[1024,128]{1,0:T(8,128)(2,1)S(1)} collective-permute-done((bf16[1024,128]{1,0:T(8,128)(2,1)}, bf16[1024,128]{1,0:T(8,128)(2,1)S(1)}, u32[]{:S(2)}, u32[]{:S(2)}) %collective-permute-start.5) | collective-permute-done | bytes 262176 | tf_op jit(solution)/shard_map/ppermute | solution.py:296
  24.6 1.5 %collective-permute-done.4.refs_1_ = bf16[1024,128]{1,0:T(8,128)(2,1)S(1)} collective-permute-done((bf16[1024,128]{1,0:T(8,128)(2,1)}, bf16[1024,128]{1,0:T(8,128)(2,1)S(1)}, u32[]{:S(2)}, u32[]{:S(2)}) %collective-permute-start.4) | collective-permute-done | bytes 262176 | tf_op jit(solution)/shard_map/ppermute | solution.py:319
  30.1 2.7 %collective-permute-done.12.refs_1_ = bf16[4,528,128]{2,1,0:T(8,128)(2,1)S(1)} collective-permute-done((bf16[4,528,128]{2,1,0:T(8,128)(2,1)S(1)}, bf16[4,528,128]{2,1,0:T(8,128)(2,1)S(1)}, u32[]{:S(2)}, u32[]{:S(2)}) %collective-permute-start.12) | collective-permute-done | bytes 540704 | tf_op jit(solution)/shard_map/ppermute | solution.py:308
  32.9 3.7 %collective-permute-done.11.refs_0_ = bf16[4,528,128]{2,1,0:T(8,128)(2,1)S(1)} collective-permute-done((bf16[4,528,128]{2,1,0:T(8,128)(2,1)S(1)}, bf16[4,528,128]{2,1,0:T(8,128)(2,1)S(1)}, u32[]{:S(2)}, u32[]{:S(2)}) %collective-permute-start.11) | collective-permute-done | bytes 540704 | tf_op jit(solution)/shard_map/ppermute | solution.py:308
  36.5 1.8 %shard_map.71 = (f32[1024,1024]{1,0:T(8,128)S(1)}, bf16[8,1024,128]{2,1,0:T(8,128)(2,1)S(1)}, f32[16,128]{1,0:T(8,128)S(1)}, f32[16,128]{1,0:T(8,128)S(1)}) custom-call(bf16[4,528,128]{2,1,0:T(8,128)(2,1)S(1)} %collective-permute-done.11.refs_0_, ...), custom_call_target="tpu_custom_call", output_to_operand_aliasing={{0}: (3, {}), {1}: (4, {})} | custom-call | tf_op jit(solution)/shard_map/pallas_call | solution.py:336
  39.3 8.2 %all_to_all.35.got_ref = f32[8,24,128]{2,1,0:T(8,128)S(1)} all-to-all(f32[8,24,128]{2,1,0:T(8,128)S(1)} %get-tuple-element.33), channel_id=1, replica_groups=mesh['row'=8,'col'=16] {'row'}, dimensions={0} | all-to-all | bytes 196608 | tf_op jit(solution)/shard_map/all_to_all | solution.py:352
  48.6 10.8 %all_to_all.36.got_ref = f32[16,24,128]{2,1,0:T(8,128)S(1)} all-to-all(f32[16,24,128]{2,1,0:T(8,128)S(1)} %shard_map.73), channel_id=1, replica_groups=mesh['row'=8,'col'=16] {'col'}, dimensions={0} | all-to-all | bytes 393216 | tf_op jit(solution)/shard_map/all_to_all | solution.py:353
  59.3 1.2 shard_map.74
  60.5 8.2 %all_to_all.37.got_ref = f32[8,24,128]{2,1,0:T(8,128)S(1)} all-to-all(f32[8,24,128]{2,1,0:T(8,128)S(1)} %shard_map.74), channel_id=1, replica_groups=mesh['row'=8,'col'=16] {'row'}, dimensions={0} | all-to-all | bytes 196608 | tf_op jit(solution)/shard_map/all_to_all | solution.py:352
  69.8 11.6 %all_to_all.38.got_ref = f32[16,24,128]{2,1,0:T(8,128)S(1)} all-to-all(f32[16,24,128]{2,1,0:T(8,128)S(1)} %shard_map.75), channel_id=1, replica_groups=mesh['row'=8,'col'=16] {'col'}, dimensions={0} | all-to-all | bytes 393216 | tf_op jit(solution)/shard_map/all_to_all | solution.py:353
  82.5 8.2 %all_to_all.39.got_ref.row_got_ref = f32[8,24,128]{2,1,0:T(8,128)S(1)} all-to-all(f32[8,24,128]{2,1,0:T(8,128)S(1)} %shard_map.76), channel_id=1, replica_groups=mesh['row'=8,'col'=16] {'row'}, dimensions={0} | all-to-all | bytes 196608 | tf_op jit(solution)/shard_map/all_to_all | solution.py:352
  90.7 3.5 %shard_map.77 = (f32[16,24,128]{2,1,0:T(8,128)S(1)}, f32[1024,1024]{1,0:T(8,128)S(1)}, f32[8,128]{1,0:T(8,128)}) custom-call(f32[8,24,128]{2,1,0:T(8,128)S(1)} %all_to_all.39.got_ref.row_got_ref, f32[1024,1024]{1,0:T(8,128)S(1)} %get-tuple-element.34.scores_ref, f32[8,128]{1,0:T(8,128)S(1)} %bitcast.8, bf16[8,1024,128]{2,1,0:T(8,128)(2,1)S(1)} %shard_map.69.refs_1_.refs_2_.t_ref), custom_call_target="tpu_custom_call" | custom-call | flops 2147483648 | tf_op jit(solution)/shard_map/pallas_call | solution.py:364
  94.2 11.6 %all_to_all.40.got_ref = f32[16,24,128]{2,1,0:T(8,128)S(1)} all-to-all(f32[16,24,128]{2,1,0:T(8,128)S(1)} %get-tuple-element.36.sent_ref), channel_id=1, replica_groups=mesh['row'=8,'col'=16] {'col'}, dimensions={0} | all-to-all | bytes 393216 | tf_op jit(solution)/shard_map/all_to_all | solution.py:353
  105.8 2.3 %shard_map.78 = (bf16[1024,1024]{1,0:T(8,128)(2,1)S(1)}, bf16[512,1024]{1,0:T(8,128)(2,1)S(1)}, f32[8,128]{1,0:T(8,128)}) custom-call(f32[16,24,128]{2,1,0:T(8,128)S(1)} %all_to_all.40.got_ref, f32[16,24,128]{2,1,0:T(8,128)S(1)} %get-tuple-element.36.sent_ref, f32[8,24,128]{2,1,0:T(8,128)S(1)} %all_to_all.39.got_ref.row_got_ref, ...), custom_call_target="tpu_custom_call" | custom-call | flops 1073741824 | tf_op jit(solution)/shard_map/pallas_call | solution.py:372
  108.2 1.3 shard_map.79.mine_ref
  109.4 1.4 %collective-permute-done.13.other_ref = bf16[512,1024]{1,0:T(8,128)(2,1)S(1)} collective-permute-done((bf16[512,1024]{1,0:T(8,128)(2,1)S(1)}, bf16[512,1024]{1,0:T(8,128)(2,1)S(1)}, u32[]{:S(2)}, u32[]{:S(2)}) %collective-permute-start.13) | collective-permute-done | bytes 1048608 | tf_op jit(solution)/shard_map/ppermute | solution.py:379
  111.0 24.0 %all_to_all.41 = bf16[64,8,1024]{2,1,0:T(8,128)(2,1)S(1)} all-to-all(bf16[64,8,1024]{2,1,0:T(8,128)(2,1)S(1)} %bitcast.5), channel_id=1, replica_groups={{0,1,2,3,4,5,6,7,8,9,10,11,12,13,14,15,32,33,34,35,36,37,38,39,40,41,42..., dimensions={0} | all-to-all | bytes 2097152 | tf_op jit(solution)/shard_map/all_to_all | solution.py:389
  (35 shorter events, 12.5 us)
Async XLA Ops:
  0.6 0.9 copy-start.1
  1.5 0.7 copy-start.3
  2.3 8.4 %collective-permute-start.2 = (bf16[528,128]{1,0:T(8,128)(2,1)S(1)}, bf16[528,128]{1,0:T(8,128)(2,1)S(1)}, u32[]{:S(2)}, u32[]{:S(2)}) collective-permute-start(bf16[528,128]{1,0:T(8,128)(2,1)S(1)} %shard_map.67.refs_0_), channel_id=1, source_target_pairs={{0,3},{1,0},{2,1},{3,2},{4,7},{5,4},{6,5},{7,6},{8,11},{9,8},{10,9... | collective-permute-start | bytes 405512 | tf_op jit(solution)/shard_map/ppermute | solution.py:308
  6.4 6.6 %collective-permute-start.1 = (bf16[528,128]{1,0:T(8,128)(2,1)S(1)}, bf16[528,128]{1,0:T(8,128)(2,1)S(1)}, u32[]{:S(2)}, u32[]{:S(2)}) collective-permute-start(bf16[528,128]{1,0:T(8,128)(2,1)S(1)} %shard_map.67.refs_0_), channel_id=1, source_target_pairs={{0,2},{1,3},{2,0},{3,1},{4,6},{5,7},{6,4},{7,5},{8,10},{9,11},{10,... | collective-permute-start | bytes 405512 | tf_op jit(solution)/shard_map/ppermute | solution.py:308
  6.4 7.7 %collective-permute-start = (bf16[528,128]{1,0:T(8,128)(2,1)S(1)}, bf16[528,128]{1,0:T(8,128)(2,1)S(1)}, u32[]{:S(2)}, u32[]{:S(2)}) collective-permute-start(bf16[528,128]{1,0:T(8,128)(2,1)S(1)} %shard_map.67.refs_0_), channel_id=1, source_target_pairs={{0,1},{1,2},{2,3},{3,0},{4,5},{5,6},{6,7},{7,4},{8,9},{9,10},{10,1... | collective-permute-start | bytes 405512 | tf_op jit(solution)/shard_map/ppermute | solution.py:308
  7.7 12.5 %collective-permute-start.9 = (bf16[1024,128]{1,0:T(8,128)(2,1)}, bf16[1024,128]{1,0:T(8,128)(2,1)S(1)}, u32[]{:S(2)}, u32[]{:S(2)}) collective-permute-start(bf16[1024,128]{1,0:T(8,128)(2,1)} %refs_0_), channel_id=1, source_target_pairs={{0,96},{16,112},{32,0},{48,16},{64,32},{80,48},{96,64},{112,80},{1... | collective-permute-start | bytes 786440 | tf_op jit(solution)/shard_map/ppermute | solution.py:296
  10.7 13.4 %collective-permute-start.5 = (bf16[1024,128]{1,0:T(8,128)(2,1)}, bf16[1024,128]{1,0:T(8,128)(2,1)S(1)}, u32[]{:S(2)}, u32[]{:S(2)}) collective-permute-start(bf16[1024,128]{1,0:T(8,128)(2,1)} %refs_0_), channel_id=1, source_target_pairs={{0,32},{16,48},{32,64},{48,80},{64,96},{80,112},{96,0},{112,16},{1... | collective-permute-start | bytes 786440 | tf_op jit(solution)/shard_map/ppermute | solution.py:296
  14.1 10.0 %collective-permute-start.7 = (bf16[1024,128]{1,0:T(8,128)(2,1)}, bf16[1024,128]{1,0:T(8,128)(2,1)S(1)}, u32[]{:S(2)}, u32[]{:S(2)}) collective-permute-start(bf16[1024,128]{1,0:T(8,128)(2,1)} %refs_0_), channel_id=1, source_target_pairs={{0,64},{16,80},{32,96},{48,112},{64,0},{80,16},{96,32},{112,48},{1... | collective-permute-start | bytes 786440 | tf_op jit(solution)/shard_map/ppermute | solution.py:296
  17.4 15.5 %collective-permute-start.12 = (bf16[4,528,128]{2,1,0:T(8,128)(2,1)S(1)}, bf16[4,528,128]{2,1,0:T(8,128)(2,1)S(1)}, u32[]{:S(2)}, u32[]{:S(2)}) collective-permute-start(bf16[4,528,128]{2,1,0:T(8,128)(2,1)S(1)} %shard_map.68.refs_0_), channel_id=1, source_target_pairs={{0,12},{1,13},{2,14},{3,15},{4,0},{5,1},{6,2},{7,3},{8,4},{9,5},{1... | collective-permute-start | bytes 1622024 | tf_op jit(solution)/shard_map/ppermute | solution.py:308
  20.2 16.4 %collective-permute-start.11 = (bf16[4,528,128]{2,1,0:T(8,128)(2,1)S(1)}, bf16[4,528,128]{2,1,0:T(8,128)(2,1)S(1)}, u32[]{:S(2)}, u32[]{:S(2)}) collective-permute-start(bf16[4,528,128]{2,1,0:T(8,128)(2,1)S(1)} %shard_map.68.refs_0_), channel_id=1, source_target_pairs={{0,4},{1,5},{2,6},{3,7},{4,8},{5,9},{6,10},{7,11},{8,12},{9,13},{1... | collective-permute-start | bytes 1622024 | tf_op jit(solution)/shard_map/ppermute | solution.py:308
  20.2 18.2 %collective-permute-start.3 = (bf16[4,528,128]{2,1,0:T(8,128)(2,1)S(1)}, bf16[4,528,128]{2,1,0:T(8,128)(2,1)S(1)}, u32[]{:S(2)}, u32[]{:S(2)}) collective-permute-start(bf16[4,528,128]{2,1,0:T(8,128)(2,1)S(1)} %shard_map.68.refs_0_), channel_id=1, source_target_pairs={{0,8},{1,9},{2,10},{3,11},{4,12},{5,13},{6,14},{7,15},{8,0},{9,1},... | collective-permute-start | bytes 1622024 | tf_op jit(solution)/shard_map/ppermute | solution.py:308
  24.1 2.0 %collective-permute-start.4 = (bf16[1024,128]{1,0:T(8,128)(2,1)}, bf16[1024,128]{1,0:T(8,128)(2,1)S(1)}, u32[]{:S(2)}, u32[]{:S(2)}) collective-permute-start(bf16[1024,128]{1,0:T(8,128)(2,1)} %refs_0_), channel_id=1, source_target_pairs={{0,16},{16,0},{32,48},{48,32},{64,80},{80,64},{96,112},{112,96},{1... | collective-permute-start | bytes 786440 | tf_op jit(solution)/shard_map/ppermute | solution.py:319
  24.1 2.2 %collective-permute-start.10 = (bf16[1024,128]{1,0:T(8,128)(2,1)S(1)}, bf16[1024,128]{1,0:T(8,128)(2,1)S(1)}, u32[]{:S(2)}, u32[]{:S(2)}) collective-permute-start(bf16[1024,128]{1,0:T(8,128)(2,1)S(1)} %collective-permute-done.9.refs_6_), channel_id=1, source_target_pairs={{0,16},{16,0},{32,48},{48,32},{64,80},{80,64},{96,112},{112,96},{1... | collective-permute-start | bytes 786440 | tf_op jit(solution)/shard_map/ppermute | solution.py:319
  26.1 1.5 %collective-permute-start.6 = (bf16[1024,128]{1,0:T(8,128)(2,1)S(1)}, bf16[1024,128]{1,0:T(8,128)(2,1)S(1)}, u32[]{:S(2)}, u32[]{:S(2)}) collective-permute-start(bf16[1024,128]{1,0:T(8,128)(2,1)S(1)} %collective-permute-done.5.refs_2_), channel_id=1, source_target_pairs={{0,16},{16,0},{32,48},{48,32},{64,80},{80,64},{96,112},{112,96},{1... | collective-permute-start | bytes 786440 | tf_op jit(solution)/shard_map/ppermute | solution.py:319
  26.3 1.8 %collective-permute-start.8 = (bf16[1024,128]{1,0:T(8,128)(2,1)S(1)}, bf16[1024,128]{1,0:T(8,128)(2,1)S(1)}, u32[]{:S(2)}, u32[]{:S(2)}) collective-permute-start(bf16[1024,128]{1,0:T(8,128)(2,1)S(1)} %collective-permute-done.7.refs_4_), channel_id=1, source_target_pairs={{0,16},{16,0},{32,48},{48,32},{64,80},{80,64},{96,112},{112,96},{1... | collective-permute-start | bytes 786440 | tf_op jit(solution)/shard_map/ppermute | solution.py:319
  28.1 1.0 copy-start
  38.3 9.2 %copy-start.2 = (f32[1024]{0:T(1024)S(1)}, f32[1024]{0:T(1024)}, u32[]{:S(2)}) copy-start(f32[1024]{0:T(1024)} %param.7) | copy-start | bytes 12292
  108.2 2.7 %collective-permute-start.13 = (bf16[512,1024]{1,0:T(8,128)(2,1)S(1)}, bf16[512,1024]{1,0:T(8,128)(2,1)S(1)}, u32[]{:S(2)}, u32[]{:S(2)}) collective-permute-start(bf16[512,1024]{1,0:T(8,128)(2,1)S(1)} %get-tuple-element.40), channel_id=1, source_target_pairs={{0,16},{16,0},{32,48},{48,32},{64,80},{80,64},{96,112},{112,96},{1... | collective-permute-start | bytes 3145736 | tf_op jit(solution)/shard_map/ppermute | solution.py:379
where the time goes:
time: 136 us
  blocking collectives  82.4 us (61%)
  starting transfers between devices  17.8 us (13%)
  Pallas kernels  15.8 us (12%)
  waiting for transfers between devices  15.7 us (12%)
  local copies, waits for them, and re-layouts  2.51 us (2%)
    all_to_all x3, blocking collectives, body(): column_swap = lambda v: lax.all_to_all(v, 'col', 0, 0)  33.9 us
    all_to_all x3, blocking collectives, body(): row_swap = lambda v: lax.all_to_all(v, 'row', 0, 0)  24.5 us
    all_to_all x1, blocking collectives, body(): lax.all_to_all(pair.reshape(count, width // 2 // count, width), ('row', '...  24 us
    ppermute x6, starting transfers between devices, shift(): return lax.ppermute(v, ('row', 'col'), moves)  10.5 us
    ppermute x6, waiting for transfers between devices, shift(): return lax.ppermute(v, ('row', 'col'), moves)  9.8 us
    ppermute x3, starting transfers between devices, back(): lax.ppermute(v, 'row', [(i, (i + cores * k) % row_count) for i in range(r...  6.29 us
    pallas_call x1, Pallas kernels, body(): call(last_row_kernel, [f32(columns, 24, LANES), f32(big, width), f32(SUB,...  3.51 us
    ppermute x4, waiting for transfers between devices, body(): lax.ppermute(piece, 'row', swap)  2.92 us
  transfers between devices with their start and end apart: 14, of which 9 were waited for; matrix products, arithmetic and copies ran while one was open for 0% of the time, Pallas kernels for 3%

commit v1 on v0

--- a/solution.py
+++ b/solution.py
@@ -274,7 +274,11 @@
     product(3)
 
 
-def second_cross_kernel(carried_ref, s_ref, out_ref):
+def second_cross_kernel(
+    carried_ref, s_ref, speech_dual_ref, text_dual_ref, out_ref, out_speech_ref, out_text_ref
+):
+    out_speech_ref[...] = speech_dual_ref[...]
+    out_text_ref[...] = text_dual_ref[...]
     out_ref[...] = half_cross(s_ref, lax.rem(lax.axis_index("row"), 2), carried_ref[...])
 
 
@@ -377,9 +381,12 @@
         args=6,
     )(got, sent, got_row, row_mass, raw, s)
     other = lax.ppermute(other, "row", swap)
-    (mine,) = call(second_cross_kernel, [f32(width // 2, width)], flops=flops // 2, args=2)(
-        carried, s
-    )
+    mine, speech_dual, text_dual = call(
+        second_cross_kernel,
+        [f32(width // 2, width), f32(SUB, LANES), f32(SUB, LANES)],
+        flops=flops // 2,
+        args=4,
+    )(carried, s, speech_dual, text_dual)
     (pair,) = call(pair_kernel, [bf16(width // 2, width)], args=2)(mine, other)
     groups = [
         [r * columns + c for r in range(core, row_count, cores) for c in range(columns)]

time: 136 us -> 135 us (level)
  transfers between devices with their start and end apart: 14 -> 14, of which waited for: 9 -> 9; matrix products, arithmetic and copies ran while one was open for 0% -> 0% of each run, Pallas kernels for 3% -> 4%
where the time goes in v1:
time: 135 us
  blocking collectives  82.4 us (61%)
  starting transfers between devices  17.8 us (13%)
  Pallas kernels  15.4 us (11%)
  waiting for transfers between devices  15.2 us (11%)
  local copies, waits for them, and re-layouts  2.51 us (2%)
    all_to_all x3, blocking collectives, body(): column_swap = lambda v: lax.all_to_all(v, 'col', 0, 0)  33.9 us
    all_to_all x3, blocking collectives, body(): row_swap = lambda v: lax.all_to_all(v, 'row', 0, 0)  24.5 us
    all_to_all x1, blocking collectives, body(): lax.all_to_all(pair.reshape(count, width // 2 // count, width), ('row', '...  23.9 us
    ppermute x6, starting transfers between devices, shift(): return lax.ppermute(v, ('row', 'col'), moves)  10.5 us
    ppermute x6, waiting for transfers between devices, shift(): return lax.ppermute(v, ('row', 'col'), moves)  9.8 us
    ppermute x3, starting transfers between devices, back(): lax.ppermute(v, 'row', [(i, (i + cores * k) % row_count) for i in range(r...  6.29 us
    pallas_call x1, Pallas kernels, body(): call(last_row_kernel, [f32(columns, 24, LANES), f32(big, width), f32(SUB,...  3.02 us
    ppermute x4, waiting for transfers between devices, body(): lax.ppermute(piece, 'row', swap)  2.92 us
  transfers between devices with their start and end apart: 14, of which 9 were waited for; matrix products, arithmetic and copies ran while one was open for 0% of the time, Pallas kernels for 4%

profile of v1, /device:TPU:0, one launch (start us, length us, event | category | flops | bytes accessed | tf_op | source)
XLA Modules:
  0.0 134.8 jit_solution(13995386509395269670)
XLA Ops:
  2.3 4.1 %collective-permute-start.2 = (bf16[528,128]{1,0:T(8,128)(2,1)S(1)}, bf16[528,128]{1,0:T(8,128)(2,1)S(1)}, u32[]{:S(2)}, u32[]{:S(2)}) collective-permute-start(bf16[528,128]{1,0:T(8,128)(2,1)S(1)} %shard_map.67.refs_0_), channel_id=1, source_target_pairs={{0,3},{1,0},{2,1},{3,2},{4,7},{5,4},{6,5},{7,6},{8,11},{9,8},{10,9... | collective-permute-start | bytes 405512 | tf_op jit(solution)/shard_map/ppermute | solution.py:312
  6.4 1.3 collective-permute-start
  7.7 3.0 %collective-permute-start.9 = (bf16[1024,128]{1,0:T(8,128)(2,1)}, bf16[1024,128]{1,0:T(8,128)(2,1)S(1)}, u32[]{:S(2)}, u32[]{:S(2)}) collective-permute-start(bf16[1024,128]{1,0:T(8,128)(2,1)} %refs_0_), channel_id=1, source_target_pairs={{0,96},{16,112},{32,0},{48,16},{64,32},{80,48},{96,64},{112,80},{1... | collective-permute-start | bytes 786440 | tf_op jit(solution)/shard_map/ppermute | solution.py:300
  10.7 2.3 %collective-permute-done.1.refs_2_ = bf16[528,128]{1,0:T(8,128)(2,1)S(1)} collective-permute-done((bf16[528,128]{1,0:T(8,128)(2,1)S(1)}, bf16[528,128]{1,0:T(8,128)(2,1)S(1)}, u32[]{:S(2)}, u32[]{:S(2)}) %collective-permute-start.1) | collective-permute-done | bytes 135200 | tf_op jit(solution)/shard_map/ppermute | solution.py:312
  14.1 3.3 %collective-permute-start.7 = (bf16[1024,128]{1,0:T(8,128)(2,1)}, bf16[1024,128]{1,0:T(8,128)(2,1)S(1)}, u32[]{:S(2)}, u32[]{:S(2)}) collective-permute-start(bf16[1024,128]{1,0:T(8,128)(2,1)} %refs_0_), channel_id=1, source_target_pairs={{0,64},{16,80},{32,96},{48,112},{64,0},{80,16},{96,32},{112,48},{1... | collective-permute-start | bytes 786440 | tf_op jit(solution)/shard_map/ppermute | solution.py:300
  17.4 2.8 %collective-permute-start.12 = (bf16[4,528,128]{2,1,0:T(8,128)(2,1)S(1)}, bf16[4,528,128]{2,1,0:T(8,128)(2,1)S(1)}, u32[]{:S(2)}, u32[]{:S(2)}) collective-permute-start(bf16[4,528,128]{2,1,0:T(8,128)(2,1)S(1)} %shard_map.68.refs_0_), channel_id=1, source_target_pairs={{0,12},{1,13},{2,14},{3,15},{4,0},{5,1},{6,2},{7,3},{8,4},{9,5},{1... | collective-permute-start | bytes 1622024 | tf_op jit(solution)/shard_map/ppermute | solution.py:312
  20.2 2.3 %collective-permute-start.3 = (bf16[4,528,128]{2,1,0:T(8,128)(2,1)S(1)}, bf16[4,528,128]{2,1,0:T(8,128)(2,1)S(1)}, u32[]{:S(2)}, u32[]{:S(2)}) collective-permute-start(bf16[4,528,128]{2,1,0:T(8,128)(2,1)S(1)} %shard_map.68.refs_0_), channel_id=1, source_target_pairs={{0,8},{1,9},{2,10},{3,11},{4,12},{5,13},{6,14},{7,15},{8,0},{9,1},... | collective-permute-start | bytes 1622024 | tf_op jit(solution)/shard_map/ppermute | solution.py:312
  22.5 1.6 %collective-permute-done.5.refs_2_ = bf16[1024,128]{1,0:T(8,128)(2,1)S(1)} collective-permute-done((bf16[1024,128]{1,0:T(8,128)(2,1)}, bf16[1024,128]{1,0:T(8,128)(2,1)S(1)}, u32[]{:S(2)}, u32[]{:S(2)}) %collective-permute-start.5) | collective-permute-done | bytes 262176 | tf_op jit(solution)/shard_map/ppermute | solution.py:300
  24.6 1.5 %collective-permute-done.4.refs_1_ = bf16[1024,128]{1,0:T(8,128)(2,1)S(1)} collective-permute-done((bf16[1024,128]{1,0:T(8,128)(2,1)}, bf16[1024,128]{1,0:T(8,128)(2,1)S(1)}, u32[]{:S(2)}, u32[]{:S(2)}) %collective-permute-start.4) | collective-permute-done | bytes 262176 | tf_op jit(solution)/shard_map/ppermute | solution.py:323
  30.1 2.7 %collective-permute-done.12.refs_1_ = bf16[4,528,128]{2,1,0:T(8,128)(2,1)S(1)} collective-permute-done((bf16[4,528,128]{2,1,0:T(8,128)(2,1)S(1)}, bf16[4,528,128]{2,1,0:T(8,128)(2,1)S(1)}, u32[]{:S(2)}, u32[]{:S(2)}) %collective-permute-start.12) | collective-permute-done | bytes 540704 | tf_op jit(solution)/shard_map/ppermute | solution.py:312
  32.9 3.7 %collective-permute-done.11.refs_0_ = bf16[4,528,128]{2,1,0:T(8,128)(2,1)S(1)} collective-permute-done((bf16[4,528,128]{2,1,0:T(8,128)(2,1)S(1)}, bf16[4,528,128]{2,1,0:T(8,128)(2,1)S(1)}, u32[]{:S(2)}, u32[]{:S(2)}) %collective-permute-start.11) | collective-permute-done | bytes 540704 | tf_op jit(solution)/shard_map/ppermute | solution.py:312
  36.5 1.8 %shard_map.71 = (f32[1024,1024]{1,0:T(8,128)S(1)}, bf16[8,1024,128]{2,1,0:T(8,128)(2,1)S(1)}, f32[16,128]{1,0:T(8,128)S(1)}, f32[16,128]{1,0:T(8,128)S(1)}) custom-call(bf16[4,528,128]{2,1,0:T(8,128)(2,1)S(1)} %collective-permute-done.11.refs_0_, ...), custom_call_target="tpu_custom_call", output_to_operand_aliasing={{0}: (3, {}), {1}: (4, {})} | custom-call | tf_op jit(solution)/shard_map/pallas_call | solution.py:340
  39.3 8.2 %all_to_all.35.got_ref = f32[8,24,128]{2,1,0:T(8,128)S(1)} all-to-all(f32[8,24,128]{2,1,0:T(8,128)S(1)} %get-tuple-element.36), channel_id=1, replica_groups=mesh['row'=8,'col'=16] {'row'}, dimensions={0} | all-to-all | bytes 196608 | tf_op jit(solution)/shard_map/all_to_all | solution.py:356
  48.6 10.8 %all_to_all.36.got_ref = f32[16,24,128]{2,1,0:T(8,128)S(1)} all-to-all(f32[16,24,128]{2,1,0:T(8,128)S(1)} %shard_map.73), channel_id=1, replica_groups=mesh['row'=8,'col'=16] {'col'}, dimensions={0} | all-to-all | bytes 393216 | tf_op jit(solution)/shard_map/all_to_all | solution.py:357
  59.3 1.2 shard_map.74
  60.5 8.2 %all_to_all.37.got_ref = f32[8,24,128]{2,1,0:T(8,128)S(1)} all-to-all(f32[8,24,128]{2,1,0:T(8,128)S(1)} %shard_map.74), channel_id=1, replica_groups=mesh['row'=8,'col'=16] {'row'}, dimensions={0} | all-to-all | bytes 196608 | tf_op jit(solution)/shard_map/all_to_all | solution.py:356
  69.8 11.6 %all_to_all.38.got_ref = f32[16,24,128]{2,1,0:T(8,128)S(1)} all-to-all(f32[16,24,128]{2,1,0:T(8,128)S(1)} %shard_map.75), channel_id=1, replica_groups=mesh['row'=8,'col'=16] {'col'}, dimensions={0} | all-to-all | bytes 393216 | tf_op jit(solution)/shard_map/all_to_all | solution.py:357
  81.4 1.2 shard_map.76
  82.6 8.2 %all_to_all.39.got_ref.row_got_ref = f32[8,24,128]{2,1,0:T(8,128)S(1)} all-to-all(f32[8,24,128]{2,1,0:T(8,128)S(1)} %shard_map.76), channel_id=1, replica_groups=mesh['row'=8,'col'=16] {'row'}, dimensions={0} | all-to-all | bytes 196608 | tf_op jit(solution)/shard_map/all_to_all | solution.py:356
  90.7 3.0 %shard_map.77 = (f32[16,24,128]{2,1,0:T(8,128)S(1)}, f32[1024,1024]{1,0:T(8,128)S(1)}, f32[8,128]{1,0:T(8,128)S(1)}) custom-call(f32[8,24,128]{2,1,0:T(8,128)S(1)} %all_to_all.39.got_ref.row_got_ref, f32[1024,1024]{1,0:T(8,128)S(1)} %get-tuple-element.37.scores_ref, f32[8,128]{1,0:T(8,128)S(1)} %bitcast.8, ...), custom_call_target="tpu_custom_call" | custom-call | flops 2147483648 | tf_op jit(solution)/shard_map/pallas_call | solution.py:368
  93.8 11.6 %all_to_all.40.got_ref = f32[16,24,128]{2,1,0:T(8,128)S(1)} all-to-all(f32[16,24,128]{2,1,0:T(8,128)S(1)} %get-tuple-element.39.sent_ref), channel_id=1, replica_groups=mesh['row'=8,'col'=16] {'col'}, dimensions={0} | all-to-all | bytes 393216 | tf_op jit(solution)/shard_map/all_to_all | solution.py:357
  105.4 1.8 %shard_map.78 = (bf16[1024,1024]{1,0:T(8,128)(2,1)S(1)}, bf16[512,1024]{1,0:T(8,128)(2,1)S(1)}, f32[8,128]{1,0:T(8,128)S(1)}) custom-call(f32[16,24,128]{2,1,0:T(8,128)S(1)} %all_to_all.40.got_ref, f32[16,24,128]{2,1,0:T(8,128)S(1)} %get-tuple-element.39.sent_ref, f32[8,24,128]{2,1,0:T(8,128)S(1)} %all_to_all.39.got_ref.row_got_ref, ...), custom_call_target="tpu_custom_call" | custom-call | flops 1073741824 | tf_op jit(solution)/shard_map/pallas_call | solution.py:376
  107.3 1.8 %shard_map.79 = (f32[512,1024]{1,0:T(8,128)S(1)}, f32[8,128]{1,0:T(8,128)}, f32[8,128]{1,0:T(8,128)}) custom-call(bf16[1024,1024]{1,0:T(8,128)(2,1)S(1)} %get-tuple-element.42.carried_ref, bf16[8,1024,128]{2,1,0:T(8,128)(2,1)S(1)} %get-tuple-element.41.s_ref, f32[8,128]{1,0:T(8,128)S(1)} %get-tuple-element.43.speech_dual_ref, ...), custom_call_target="tpu_custom_call" | custom-call | flops 1073741824 | tf_op jit(solution)/shard_map/pallas_call | solution.py:384
  110.1 23.9 %all_to_all.41 = bf16[64,8,1024]{2,1,0:T(8,128)(2,1)S(1)} all-to-all(bf16[64,8,1024]{2,1,0:T(8,128)(2,1)S(1)} %bitcast.5), channel_id=1, replica_groups={{0,1,2,3,4,5,6,7,8,9,10,11,12,13,14,15,32,33,34,35,36,37,38,39,40,41,42..., dimensions={0} | all-to-all | bytes 2097152 | tf_op jit(solution)/shard_map/all_to_all | solution.py:396
  (35 shorter events, 12.3 us)
Async XLA Ops:
  0.6 0.9 copy-start.1
  1.5 0.7 copy-start.3
  2.3 8.4 %collective-permute-start.2 = (bf16[528,128]{1,0:T(8,128)(2,1)S(1)}, bf16[528,128]{1,0:T(8,128)(2,1)S(1)}, u32[]{:S(2)}, u32[]{:S(2)}) collective-permute-start(bf16[528,128]{1,0:T(8,128)(2,1)S(1)} %shard_map.67.refs_0_), channel_id=1, source_target_pairs={{0,3},{1,0},{2,1},{3,2},{4,7},{5,4},{6,5},{7,6},{8,11},{9,8},{10,9... | collective-permute-start | bytes 405512 | tf_op jit(solution)/shard_map/ppermute | solution.py:312
  6.4 6.6 %collective-permute-start.1 = (bf16[528,128]{1,0:T(8,128)(2,1)S(1)}, bf16[528,128]{1,0:T(8,128)(2,1)S(1)}, u32[]{:S(2)}, u32[]{:S(2)}) collective-permute-start(bf16[528,128]{1,0:T(8,128)(2,1)S(1)} %shard_map.67.refs_0_), channel_id=1, source_target_pairs={{0,2},{1,3},{2,0},{3,1},{4,6},{5,7},{6,4},{7,5},{8,10},{9,11},{10,... | collective-permute-start | bytes 405512 | tf_op jit(solution)/shard_map/ppermute | solution.py:312
  6.4 7.7 %collective-permute-start = (bf16[528,128]{1,0:T(8,128)(2,1)S(1)}, bf16[528,128]{1,0:T(8,128)(2,1)S(1)}, u32[]{:S(2)}, u32[]{:S(2)}) collective-permute-start(bf16[528,128]{1,0:T(8,128)(2,1)S(1)} %shard_map.67.refs_0_), channel_id=1, source_target_pairs={{0,1},{1,2},{2,3},{3,0},{4,5},{5,6},{6,7},{7,4},{8,9},{9,10},{10,1... | collective-permute-start | bytes 405512 | tf_op jit(solution)/shard_map/ppermute | solution.py:312
  7.7 12.5 %collective-permute-start.9 = (bf16[1024,128]{1,0:T(8,128)(2,1)}, bf16[1024,128]{1,0:T(8,128)(2,1)S(1)}, u32[]{:S(2)}, u32[]{:S(2)}) collective-permute-start(bf16[1024,128]{1,0:T(8,128)(2,1)} %refs_0_), channel_id=1, source_target_pairs={{0,96},{16,112},{32,0},{48,16},{64,32},{80,48},{96,64},{112,80},{1... | collective-permute-start | bytes 786440 | tf_op jit(solution)/shard_map/ppermute | solution.py:300
  10.7 13.4 %collective-permute-start.5 = (bf16[1024,128]{1,0:T(8,128)(2,1)}, bf16[1024,128]{1,0:T(8,128)(2,1)S(1)}, u32[]{:S(2)}, u32[]{:S(2)}) collective-permute-start(bf16[1024,128]{1,0:T(8,128)(2,1)} %refs_0_), channel_id=1, source_target_pairs={{0,32},{16,48},{32,64},{48,80},{64,96},{80,112},{96,0},{112,16},{1... | collective-permute-start | bytes 786440 | tf_op jit(solution)/shard_map/ppermute | solution.py:300
  14.1 10.0 %collective-permute-start.7 = (bf16[1024,128]{1,0:T(8,128)(2,1)}, bf16[1024,128]{1,0:T(8,128)(2,1)S(1)}, u32[]{:S(2)}, u32[]{:S(2)}) collective-permute-start(bf16[1024,128]{1,0:T(8,128)(2,1)} %refs_0_), channel_id=1, source_target_pairs={{0,64},{16,80},{32,96},{48,112},{64,0},{80,16},{96,32},{112,48},{1... | collective-permute-start | bytes 786440 | tf_op jit(solution)/shard_map/ppermute | solution.py:300
  17.4 15.5 %collective-permute-start.12 = (bf16[4,528,128]{2,1,0:T(8,128)(2,1)S(1)}, bf16[4,528,128]{2,1,0:T(8,128)(2,1)S(1)}, u32[]{:S(2)}, u32[]{:S(2)}) collective-permute-start(bf16[4,528,128]{2,1,0:T(8,128)(2,1)S(1)} %shard_map.68.refs_0_), channel_id=1, source_target_pairs={{0,12},{1,13},{2,14},{3,15},{4,0},{5,1},{6,2},{7,3},{8,4},{9,5},{1... | collective-permute-start | bytes 1622024 | tf_op jit(solution)/shard_map/ppermute | solution.py:312
  20.2 16.4 %collective-permute-start.11 = (bf16[4,528,128]{2,1,0:T(8,128)(2,1)S(1)}, bf16[4,528,128]{2,1,0:T(8,128)(2,1)S(1)}, u32[]{:S(2)}, u32[]{:S(2)}) collective-permute-start(bf16[4,528,128]{2,1,0:T(8,128)(2,1)S(1)} %shard_map.68.refs_0_), channel_id=1, source_target_pairs={{0,4},{1,5},{2,6},{3,7},{4,8},{5,9},{6,10},{7,11},{8,12},{9,13},{1... | collective-permute-start | bytes 1622024 | tf_op jit(solution)/shard_map/ppermute | solution.py:312
  20.2 18.2 %collective-permute-start.3 = (bf16[4,528,128]{2,1,0:T(8,128)(2,1)S(1)}, bf16[4,528,128]{2,1,0:T(8,128)(2,1)S(1)}, u32[]{:S(2)}, u32[]{:S(2)}) collective-permute-start(bf16[4,528,128]{2,1,0:T(8,128)(2,1)S(1)} %shard_map.68.refs_0_), channel_id=1, source_target_pairs={{0,8},{1,9},{2,10},{3,11},{4,12},{5,13},{6,14},{7,15},{8,0},{9,1},... | collective-permute-start | bytes 1622024 | tf_op jit(solution)/shard_map/ppermute | solution.py:312
  24.1 2.0 %collective-permute-start.4 = (bf16[1024,128]{1,0:T(8,128)(2,1)}, bf16[1024,128]{1,0:T(8,128)(2,1)S(1)}, u32[]{:S(2)}, u32[]{:S(2)}) collective-permute-start(bf16[1024,128]{1,0:T(8,128)(2,1)} %refs_0_), channel_id=1, source_target_pairs={{0,16},{16,0},{32,48},{48,32},{64,80},{80,64},{96,112},{112,96},{1... | collective-permute-start | bytes 786440 | tf_op jit(solution)/shard_map/ppermute | solution.py:323
  24.1 2.2 %collective-permute-start.10 = (bf16[1024,128]{1,0:T(8,128)(2,1)S(1)}, bf16[1024,128]{1,0:T(8,128)(2,1)S(1)}, u32[]{:S(2)}, u32[]{:S(2)}) collective-permute-start(bf16[1024,128]{1,0:T(8,128)(2,1)S(1)} %collective-permute-done.9.refs_6_), channel_id=1, source_target_pairs={{0,16},{16,0},{32,48},{48,32},{64,80},{80,64},{96,112},{112,96},{1... | collective-permute-start | bytes 786440 | tf_op jit(solution)/shard_map/ppermute | solution.py:323
  26.1 1.5 %collective-permute-start.6 = (bf16[1024,128]{1,0:T(8,128)(2,1)S(1)}, bf16[1024,128]{1,0:T(8,128)(2,1)S(1)}, u32[]{:S(2)}, u32[]{:S(2)}) collective-permute-start(bf16[1024,128]{1,0:T(8,128)(2,1)S(1)} %collective-permute-done.5.refs_2_), channel_id=1, source_target_pairs={{0,16},{16,0},{32,48},{48,32},{64,80},{80,64},{96,112},{112,96},{1... | collective-permute-start | bytes 786440 | tf_op jit(solution)/shard_map/ppermute | solution.py:323
  26.3 1.8 %collective-permute-start.8 = (bf16[1024,128]{1,0:T(8,128)(2,1)S(1)}, bf16[1024,128]{1,0:T(8,128)(2,1)S(1)}, u32[]{:S(2)}, u32[]{:S(2)}) collective-permute-start(bf16[1024,128]{1,0:T(8,128)(2,1)S(1)} %collective-permute-done.7.refs_4_), channel_id=1, source_target_pairs={{0,16},{16,0},{32,48},{48,32},{64,80},{80,64},{96,112},{112,96},{1... | collective-permute-start | bytes 786440 | tf_op jit(solution)/shard_map/ppermute | solution.py:323
  28.1 1.0 copy-start
  38.3 9.2 %copy-start.2 = (f32[1024]{0:T(1024)S(1)}, f32[1024]{0:T(1024)}, u32[]{:S(2)}) copy-start(f32[1024]{0:T(1024)} %param.7) | copy-start | bytes 12292
  107.2 2.7 %collective-permute-start.13 = (bf16[512,1024]{1,0:T(8,128)(2,1)S(1)}, bf16[512,1024]{1,0:T(8,128)(2,1)S(1)}, u32[]{:S(2)}, u32[]{:S(2)}) collective-permute-start(bf16[512,1024]{1,0:T(8,128)(2,1)S(1)} %get-tuple-element.46), channel_id=1, source_target_pairs={{0,16},{16,0},{32,48},{48,32},{64,80},{80,64},{96,112},{112,96},{1... | collective-permute-start | bytes 3145736 | tf_op jit(solution)/shard_map/ppermute | solution.py:383

commit v2 on v1

--- a/solution.py
+++ b/solution.py
@@ -113,6 +113,10 @@
     chips = blocks // 2
     for k in range(blocks):
         t_ref[lax.rem(here // 2 + chips - k // 2, chips) * 2 + lax.rem(here + k, 2)] = slice_refs[k][...]
+
+
+def stage_kernel(text_ref, out_ref):
+    out_ref[...] = text_ref[...]
 
 
 def join_kernel(*refs):
@@ -321,6 +325,8 @@
     lines = [line] + [shift(line, k, 1) for k in range(1, side)]
     slices = [late, beside[0], back(late, 2), beside[1]]
     slices = [v for piece in slices for v in (piece, lax.ppermute(piece, "row", swap))]
+    own, slices[4] = lax.optimization_barrier((text, slices[4]))
+    (slices[0],) = call(stage_kernel, [bf16(*text.shape)], args=1)(own)
     column_mass = text_mass.reshape(SUB, LANES)
 
     scale = LOG2E / (math.sqrt(width) * EPS)

time: 135 us -> 134 us (level)
  waiting for transfers between devices: 15.2 us -> 12.5 us
  blocking collectives: 82.4 us -> 84.3 us
    ppermute x6, waiting for transfers between devices: 9.8 us -> 6.34 us  [shift(): return lax.ppermute(v, ('row', 'col'), moves)]
    ppermute x3, waiting for transfers between devices: 1.65 us -> 4.89 us  [back(): lax.ppermute(v, 'row', [(i, (i + cores * k) % row_count) for i in range(r...]
    ppermute x4, waiting for transfers between devices: 2.92 us -> 0.43 us  [body(): lax.ppermute(piece, 'row', swap)]
    all_to_all x3, blocking collectives: 24.5 us -> 26.4 us  [body(): row_swap = lambda v: lax.all_to_all(v, 'row', 0, 0)]
  transfers between devices with their start and end apart: 14 -> 14, of which waited for: 9 -> 6; matrix products, arithmetic and copies ran while one was open for 0% -> 0% of each run, Pallas kernels for 4% -> 4%
where the time goes in v2:
time: 134 us
  blocking collectives  84.3 us (63%)
  starting transfers between devices  17.4 us (13%)
  Pallas kernels  15.4 us (11%)
  waiting for transfers between devices  12.5 us (9%)
  local copies, waits for them, and re-layouts  2.51 us (2%)
    all_to_all x3, blocking collectives, body(): column_swap = lambda v: lax.all_to_all(v, 'col', 0, 0)  34 us
    all_to_all x3, blocking collectives, body(): row_swap = lambda v: lax.all_to_all(v, 'row', 0, 0)  26.4 us
    all_to_all x1, blocking collectives, body(): lax.all_to_all(pair.reshape(count, width // 2 // count, width), ('row', '...  23.9 us
    ppermute x6, starting transfers between devices, shift(): return lax.ppermute(v, ('row', 'col'), moves)  10.5 us
    ppermute x6, waiting for transfers between devices, shift(): return lax.ppermute(v, ('row', 'col'), moves)  6.34 us
    ppermute x3, starting transfers between devices, back(): lax.ppermute(v, 'row', [(i, (i + cores * k) % row_count) for i in range(r...  6.21 us
    ppermute x3, waiting for transfers between devices, back(): lax.ppermute(v, 'row', [(i, (i + cores * k) % row_count) for i in range(r...  4.89 us
    pallas_call x1, Pallas kernels, body(): call(last_row_kernel, [f32(columns, 24, LANES), f32(big, width), f32(SUB,...  3.02 us
  transfers between devices with their start and end apart: 14, of which 6 were waited for; matrix products, arithmetic and copies ran while one was open for 0% of the time, Pallas kernels for 4%

profile of v2, /device:TPU:0, one launch (start us, length us, event | category | flops | bytes accessed | tf_op | source)
XLA Modules:
  0.0 133.7 jit_solution(6840545175609248088)
XLA Ops:
  2.3 4.1 %collective-permute-start.2 = (bf16[528,128]{1,0:T(8,128)(2,1)S(1)}, bf16[528,128]{1,0:T(8,128)(2,1)S(1)}, u32[]{:S(2)}, u32[]{:S(2)}) collective-permute-start(bf16[528,128]{1,0:T(8,128)(2,1)S(1)} %shard_map.67.refs_0_), channel_id=1, source_target_pairs={{0,3},{1,0},{2,1},{3,2},{4,7},{5,4},{6,5},{7,6},{8,11},{9,8},{10,9... | collective-permute-start | bytes 405512 | tf_op jit(solution)/shard_map/ppermute | solution.py:316
  6.4 1.3 collective-permute-start
  7.7 3.0 %collective-permute-start.9 = (bf16[1024,128]{1,0:T(8,128)(2,1)}, bf16[1024,128]{1,0:T(8,128)(2,1)S(1)}, u32[]{:S(2)}, u32[]{:S(2)}) collective-permute-start(bf16[1024,128]{1,0:T(8,128)(2,1)} %text_ref), channel_id=1, source_target_pairs={{0,96},{16,112},{32,0},{48,16},{64,32},{80,48},{96,64},{112,80},{1... | collective-permute-start | bytes 786440 | tf_op jit(solution)/shard_map/ppermute | solution.py:304
  10.7 2.3 %collective-permute-done.1.refs_2_ = bf16[528,128]{1,0:T(8,128)(2,1)S(1)} collective-permute-done((bf16[528,128]{1,0:T(8,128)(2,1)S(1)}, bf16[528,128]{1,0:T(8,128)(2,1)S(1)}, u32[]{:S(2)}, u32[]{:S(2)}) %collective-permute-start.1) | collective-permute-done | bytes 135200 | tf_op jit(solution)/shard_map/ppermute | solution.py:316
  14.2 2.8 %collective-permute-start.12 = (bf16[4,528,128]{2,1,0:T(8,128)(2,1)S(1)}, bf16[4,528,128]{2,1,0:T(8,128)(2,1)S(1)}, u32[]{:S(2)}, u32[]{:S(2)}) collective-permute-start(bf16[4,528,128]{2,1,0:T(8,128)(2,1)S(1)} %shard_map.68.refs_0_), channel_id=1, source_target_pairs={{0,12},{1,13},{2,14},{3,15},{4,0},{5,1},{6,2},{7,3},{8,4},{9,5},{1... | collective-permute-start | bytes 1622024 | tf_op jit(solution)/shard_map/ppermute | solution.py:316
  17.1 2.3 %collective-permute-start.3 = (bf16[4,528,128]{2,1,0:T(8,128)(2,1)S(1)}, bf16[4,528,128]{2,1,0:T(8,128)(2,1)S(1)}, u32[]{:S(2)}, u32[]{:S(2)}) collective-permute-start(bf16[4,528,128]{2,1,0:T(8,128)(2,1)S(1)} %shard_map.68.refs_0_), channel_id=1, source_target_pairs={{0,8},{1,9},{2,10},{3,11},{4,12},{5,13},{6,14},{7,15},{8,0},{9,1},... | collective-permute-start | bytes 1622024 | tf_op jit(solution)/shard_map/ppermute | solution.py:316
  19.4 3.2 %collective-permute-start.4 = (bf16[1024,128]{1,0:T(8,128)(2,1)}, bf16[1024,128]{1,0:T(8,128)(2,1)S(1)}, u32[]{:S(2)}, u32[]{:S(2)}) collective-permute-start(bf16[1024,128]{1,0:T(8,128)(2,1)} %text_ref), channel_id=1, source_target_pairs={{0,64},{16,80},{32,96},{48,112},{64,0},{80,16},{96,32},{112,48},{1... | collective-permute-start | bytes 786440 | tf_op jit(solution)/shard_map/ppermute | solution.py:304
  22.6 4.9 %collective-permute-done.4.refs_4_ = bf16[1024,128]{1,0:T(8,128)(2,1)S(1)} collective-permute-done((bf16[1024,128]{1,0:T(8,128)(2,1)}, bf16[1024,128]{1,0:T(8,128)(2,1)S(1)}, u32[]{:S(2)}, u32[]{:S(2)}) %collective-permute-start.4) | collective-permute-done | bytes 262176 | tf_op jit(solution)/shard_map/ppermute | solution.py:304
  30.5 2.9 %collective-permute-done.11.refs_0_ = bf16[4,528,128]{2,1,0:T(8,128)(2,1)S(1)} collective-permute-done((bf16[4,528,128]{2,1,0:T(8,128)(2,1)S(1)}, bf16[4,528,128]{2,1,0:T(8,128)(2,1)S(1)}, u32[]{:S(2)}, u32[]{:S(2)}) %collective-permute-start.11) | collective-permute-done | bytes 540704 | tf_op jit(solution)/shard_map/ppermute | solution.py:316
  33.4 1.8 %shard_map.72 = (f32[1024,1024]{1,0:T(8,128)S(1)}, bf16[8,1024,128]{2,1,0:T(8,128)(2,1)S(1)}, f32[16,128]{1,0:T(8,128)S(1)}, f32[16,128]{1,0:T(8,128)S(1)}) custom-call(bf16[4,528,128]{2,1,0:T(8,128)(2,1)S(1)} %collective-permute-done.11.refs_0_, ...), custom_call_target="tpu_custom_call", output_to_operand_aliasing={{0}: (3, {}), {1}: (4, {})} | custom-call | tf_op jit(solution)/shard_map/pallas_call | solution.py:346
  36.2 10.1 %all_to_all.35.got_ref = f32[8,24,128]{2,1,0:T(8,128)S(1)} all-to-all(f32[8,24,128]{2,1,0:T(8,128)S(1)} %get-tuple-element.40), channel_id=1, replica_groups=mesh['row'=8,'col'=16] {'row'}, dimensions={0} | all-to-all | bytes 196608 | tf_op jit(solution)/shard_map/all_to_all | solution.py:362
  46.3 1.1 shard_map.74
  47.4 10.8 %all_to_all.36.got_ref = f32[16,24,128]{2,1,0:T(8,128)S(1)} all-to-all(f32[16,24,128]{2,1,0:T(8,128)S(1)} %shard_map.74), channel_id=1, replica_groups=mesh['row'=8,'col'=16] {'col'}, dimensions={0} | all-to-all | bytes 393216 | tf_op jit(solution)/shard_map/all_to_all | solution.py:363
  58.2 1.2 shard_map.75
  59.4 8.2 %all_to_all.37.got_ref = f32[8,24,128]{2,1,0:T(8,128)S(1)} all-to-all(f32[8,24,128]{2,1,0:T(8,128)S(1)} %shard_map.75), channel_id=1, replica_groups=mesh['row'=8,'col'=16] {'row'}, dimensions={0} | all-to-all | bytes 196608 | tf_op jit(solution)/shard_map/all_to_all | solution.py:362
  67.5 1.1 shard_map.76
  68.6 11.6 %all_to_all.38.got_ref = f32[16,24,128]{2,1,0:T(8,128)S(1)} all-to-all(f32[16,24,128]{2,1,0:T(8,128)S(1)} %shard_map.76), channel_id=1, replica_groups=mesh['row'=8,'col'=16] {'col'}, dimensions={0} | all-to-all | bytes 393216 | tf_op jit(solution)/shard_map/all_to_all | solution.py:363
  80.2 1.2 shard_map.77
  81.4 8.2 %all_to_all.39.got_ref.row_got_ref = f32[8,24,128]{2,1,0:T(8,128)S(1)} all-to-all(f32[8,24,128]{2,1,0:T(8,128)S(1)} %shard_map.77), channel_id=1, replica_groups=mesh['row'=8,'col'=16] {'row'}, dimensions={0} | all-to-all | bytes 196608 | tf_op jit(solution)/shard_map/all_to_all | solution.py:362
  89.6 3.0 %shard_map.78 = (f32[16,24,128]{2,1,0:T(8,128)S(1)}, f32[1024,1024]{1,0:T(8,128)S(1)}, f32[8,128]{1,0:T(8,128)S(1)}) custom-call(f32[8,24,128]{2,1,0:T(8,128)S(1)} %all_to_all.39.got_ref.row_got_ref, f32[1024,1024]{1,0:T(8,128)S(1)} %get-tuple-element.41.scores_ref, f32[8,128]{1,0:T(8,128)S(1)} %bitcast.8, ...), custom_call_target="tpu_custom_call" | custom-call | flops 2147483648 | tf_op jit(solution)/shard_map/pallas_call | solution.py:374
  92.6 11.6 %all_to_all.40.got_ref = f32[16,24,128]{2,1,0:T(8,128)S(1)} all-to-all(f32[16,24,128]{2,1,0:T(8,128)S(1)} %get-tuple-element.43.sent_ref), channel_id=1, replica_groups=mesh['row'=8,'col'=16] {'col'}, dimensions={0} | all-to-all | bytes 393216 | tf_op jit(solution)/shard_map/all_to_all | solution.py:363
  104.2 1.8 %shard_map.79 = (bf16[1024,1024]{1,0:T(8,128)(2,1)S(1)}, bf16[512,1024]{1,0:T(8,128)(2,1)S(1)}, f32[8,128]{1,0:T(8,128)S(1)}) custom-call(f32[16,24,128]{2,1,0:T(8,128)S(1)} %all_to_all.40.got_ref, f32[16,24,128]{2,1,0:T(8,128)S(1)} %get-tuple-element.43.sent_ref, f32[8,24,128]{2,1,0:T(8,128)S(1)} %all_to_all.39.got_ref.row_got_ref, ...), custom_call_target="tpu_custom_call" | custom-call | flops 1073741824 | tf_op jit(solution)/shard_map/pallas_call | solution.py:382
  106.1 1.8 %shard_map.80 = (f32[512,1024]{1,0:T(8,128)S(1)}, f32[8,128]{1,0:T(8,128)}, f32[8,128]{1,0:T(8,128)}) custom-call(bf16[1024,1024]{1,0:T(8,128)(2,1)S(1)} %get-tuple-element.46.carried_ref, bf16[8,1024,128]{2,1,0:T(8,128)(2,1)S(1)} %get-tuple-element.45.s_ref, f32[8,128]{1,0:T(8,128)S(1)} %get-tuple-element.47.speech_dual_ref, ...), custom_call_target="tpu_custom_call" | custom-call | flops 1073741824 | tf_op jit(solution)/shard_map/pallas_call | solution.py:390
  108.9 23.9 %all_to_all.41 = bf16[64,8,1024]{2,1,0:T(8,128)(2,1)S(1)} all-to-all(bf16[64,8,1024]{2,1,0:T(8,128)(2,1)S(1)} %bitcast.5), channel_id=1, replica_groups={{0,1,2,3,4,5,6,7,8,9,10,11,12,13,14,15,32,33,34,35,36,37,38,39,40,41,42..., dimensions={0} | all-to-all | bytes 2097152 | tf_op jit(solution)/shard_map/all_to_all | solution.py:402
  (36 shorter events, 8.7 us)
Async XLA Ops:
  0.6 0.9 copy-start.1
  1.5 0.7 copy-start.3
  2.3 8.4 %collective-permute-start.2 = (bf16[528,128]{1,0:T(8,128)(2,1)S(1)}, bf16[528,128]{1,0:T(8,128)(2,1)S(1)}, u32[]{:S(2)}, u32[]{:S(2)}) collective-permute-start(bf16[528,128]{1,0:T(8,128)(2,1)S(1)} %shard_map.67.refs_0_), channel_id=1, source_target_pairs={{0,3},{1,0},{2,1},{3,2},{4,7},{5,4},{6,5},{7,6},{8,11},{9,8},{10,9... | collective-permute-start | bytes 405512 | tf_op jit(solution)/shard_map/ppermute | solution.py:316
  6.4 6.6 %collective-permute-start.1 = (bf16[528,128]{1,0:T(8,128)(2,1)S(1)}, bf16[528,128]{1,0:T(8,128)(2,1)S(1)}, u32[]{:S(2)}, u32[]{:S(2)}) collective-permute-start(bf16[528,128]{1,0:T(8,128)(2,1)S(1)} %shard_map.67.refs_0_), channel_id=1, source_target_pairs={{0,2},{1,3},{2,0},{3,1},{4,6},{5,7},{6,4},{7,5},{8,10},{9,11},{10,... | collective-permute-start | bytes 405512 | tf_op jit(solution)/shard_map/ppermute | solution.py:316
  6.4 7.7 %collective-permute-start = (bf16[528,128]{1,0:T(8,128)(2,1)S(1)}, bf16[528,128]{1,0:T(8,128)(2,1)S(1)}, u32[]{:S(2)}, u32[]{:S(2)}) collective-permute-start(bf16[528,128]{1,0:T(8,128)(2,1)S(1)} %shard_map.67.refs_0_), channel_id=1, source_target_pairs={{0,1},{1,2},{2,3},{3,0},{4,5},{5,6},{6,7},{7,4},{8,9},{9,10},{10,1... | collective-permute-start | bytes 405512 | tf_op jit(solution)/shard_map/ppermute | solution.py:316
  7.7 9.4 %collective-permute-start.9 = (bf16[1024,128]{1,0:T(8,128)(2,1)}, bf16[1024,128]{1,0:T(8,128)(2,1)S(1)}, u32[]{:S(2)}, u32[]{:S(2)}) collective-permute-start(bf16[1024,128]{1,0:T(8,128)(2,1)} %text_ref), channel_id=1, source_target_pairs={{0,96},{16,112},{32,0},{48,16},{64,32},{80,48},{96,64},{112,80},{1... | collective-permute-start | bytes 786440 | tf_op jit(solution)/shard_map/ppermute | solution.py:304
  10.7 8.7 %collective-permute-start.6 = (bf16[1024,128]{1,0:T(8,128)(2,1)}, bf16[1024,128]{1,0:T(8,128)(2,1)S(1)}, u32[]{:S(2)}, u32[]{:S(2)}) collective-permute-start(bf16[1024,128]{1,0:T(8,128)(2,1)} %text_ref), channel_id=1, source_target_pairs={{0,32},{16,48},{32,64},{48,80},{64,96},{80,112},{96,0},{112,16},{1... | collective-permute-start | bytes 786440 | tf_op jit(solution)/shard_map/ppermute | solution.py:304
  14.1 8.4 %collective-permute-start.5 = (bf16[1024,128]{1,0:T(8,128)(2,1)}, bf16[1024,128]{1,0:T(8,128)(2,1)S(1)}, u32[]{:S(2)}, u32[]{:S(2)}) collective-permute-start(bf16[1024,128]{1,0:T(8,128)(2,1)} %text_ref), channel_id=1, source_target_pairs={{0,16},{16,0},{32,48},{48,32},{64,80},{80,64},{96,112},{112,96},{1... | collective-permute-start | bytes 786440 | tf_op jit(solution)/shard_map/ppermute | solution.py:327
  14.2 16.2 %collective-permute-start.12 = (bf16[4,528,128]{2,1,0:T(8,128)(2,1)S(1)}, bf16[4,528,128]{2,1,0:T(8,128)(2,1)S(1)}, u32[]{:S(2)}, u32[]{:S(2)}) collective-permute-start(bf16[4,528,128]{2,1,0:T(8,128)(2,1)S(1)} %shard_map.68.refs_0_), channel_id=1, source_target_pairs={{0,12},{1,13},{2,14},{3,15},{4,0},{5,1},{6,2},{7,3},{8,4},{9,5},{1... | collective-permute-start | bytes 1622024 | tf_op jit(solution)/shard_map/ppermute | solution.py:316
  17.1 16.4 %collective-permute-start.11 = (bf16[4,528,128]{2,1,0:T(8,128)(2,1)S(1)}, bf16[4,528,128]{2,1,0:T(8,128)(2,1)S(1)}, u32[]{:S(2)}, u32[]{:S(2)}) collective-permute-start(bf16[4,528,128]{2,1,0:T(8,128)(2,1)S(1)} %shard_map.68.refs_0_), channel_id=1, source_target_pairs={{0,4},{1,5},{2,6},{3,7},{4,8},{5,9},{6,10},{7,11},{8,12},{9,13},{1... | collective-permute-start | bytes 1622024 | tf_op jit(solution)/shard_map/ppermute | solution.py:316
  17.1 18.2 %collective-permute-start.3 = (bf16[4,528,128]{2,1,0:T(8,128)(2,1)S(1)}, bf16[4,528,128]{2,1,0:T(8,128)(2,1)S(1)}, u32[]{:S(2)}, u32[]{:S(2)}) collective-permute-start(bf16[4,528,128]{2,1,0:T(8,128)(2,1)S(1)} %shard_map.68.refs_0_), channel_id=1, source_target_pairs={{0,8},{1,9},{2,10},{3,11},{4,12},{5,13},{6,14},{7,15},{8,0},{9,1},... | collective-permute-start | bytes 1622024 | tf_op jit(solution)/shard_map/ppermute | solution.py:316
  19.4 8.1 %collective-permute-start.4 = (bf16[1024,128]{1,0:T(8,128)(2,1)}, bf16[1024,128]{1,0:T(8,128)(2,1)S(1)}, u32[]{:S(2)}, u32[]{:S(2)}) collective-permute-start(bf16[1024,128]{1,0:T(8,128)(2,1)} %text_ref), channel_id=1, source_target_pairs={{0,64},{16,80},{32,96},{48,112},{64,0},{80,16},{96,32},{112,48},{1... | collective-permute-start | bytes 786440 | tf_op jit(solution)/shard_map/ppermute | solution.py:304
  22.6 4.9 %collective-permute-start.10 = (bf16[1024,128]{1,0:T(8,128)(2,1)S(1)}, bf16[1024,128]{1,0:T(8,128)(2,1)S(1)}, u32[]{:S(2)}, u32[]{:S(2)}) collective-permute-start(bf16[1024,128]{1,0:T(8,128)(2,1)S(1)} %collective-permute-done.9.refs_6_), channel_id=1, source_target_pairs={{0,16},{16,0},{32,48},{48,32},{64,80},{80,64},{96,112},{112,96},{1... | collective-permute-start | bytes 786440 | tf_op jit(solution)/shard_map/ppermute | solution.py:327
  27.4 1.5 %collective-permute-start.7 = (bf16[1024,128]{1,0:T(8,128)(2,1)S(1)}, bf16[1024,128]{1,0:T(8,128)(2,1)S(1)}, u32[]{:S(2)}, u32[]{:S(2)}) collective-permute-start(bf16[1024,128]{1,0:T(8,128)(2,1)S(1)} %collective-permute-done.6.refs_2_), channel_id=1, source_target_pairs={{0,16},{16,0},{32,48},{48,32},{64,80},{80,64},{96,112},{112,96},{1... | collective-permute-start | bytes 786440 | tf_op jit(solution)/shard_map/ppermute | solution.py:327
  27.4 1.9 %collective-permute-start.8 = (bf16[1024,128]{1,0:T(8,128)(2,1)S(1)}, bf16[1024,128]{1,0:T(8,128)(2,1)S(1)}, u32[]{:S(2)}, u32[]{:S(2)}) collective-permute-start(bf16[1024,128]{1,0:T(8,128)(2,1)S(1)} %collective-permute-done.4.refs_4_), channel_id=1, source_target_pairs={{0,16},{16,0},{32,48},{48,32},{64,80},{80,64},{96,112},{112,96},{1... | collective-permute-start | bytes 786440 | tf_op jit(solution)/shard_map/ppermute | solution.py:327
  28.0 0.9 copy-start
  35.2 11.1 %copy-start.2 = (f32[1024]{0:T(1024)S(1)}, f32[1024]{0:T(1024)}, u32[]{:S(2)}) copy-start(f32[1024]{0:T(1024)} %param.7) | copy-start | bytes 12292
  106.0 2.7 %collective-permute-start.13 = (bf16[512,1024]{1,0:T(8,128)(2,1)S(1)}, bf16[512,1024]{1,0:T(8,128)(2,1)S(1)}, u32[]{:S(2)}, u32[]{:S(2)}) collective-permute-start(bf16[512,1024]{1,0:T(8,128)(2,1)S(1)} %get-tuple-element.50), channel_id=1, source_target_pairs={{0,16},{16,0},{32,48},{48,32},{64,80},{80,64},{96,112},{112,96},{1... | collective-permute-start | bytes 3145736 | tf_op jit(solution)/shard_map/ppermute | solution.py:389
